TPU v7x, 32 devices: a whole 2x2x4 slice. The times are simulated.
32 devices in a mesh: seqlo: 8 (over z, y), seqhi: 4 (over x, core).
Axes of the slice: x: 2, y: 2, z: 4, core: 2. Of those that a mesh axis runs over, the one named last changes fastest.
Arguments:
- waveform_input: bfloat16 [65536, 256], P(('seqhi', 'seqlo')), may hold values from -6 to 6
- first_conv_weight: bfloat16 [512, 512], P('seqhi'), may hold values from -0.25 to 0.25
- first_projection_weight: bfloat16 [256, 256], P('seqhi'), may hold values from -0.375 to 0.375
- second_conv_weight: bfloat16 [512, 512], P('seqhi'), may hold values from -0.25 to 0.25
- second_projection_weight: bfloat16 [256, 256], P('seqhi'), may hold values from -0.375 to 0.375
- final_cotangent: bfloat16 [65536, 256], P(('seqhi', 'seqlo')), may hold values from -6 to 6
Outputs:
- input_cotangent: bfloat16 [65536, 256], P(('seqhi', 'seqlo'))
- first_conv_gradient: float32 [512, 512], P('seqhi')
- first_projection_gradient: float32 [256, 256], P('seqhi')
- second_conv_gradient: float32 [512, 512], P('seqhi')
- second_projection_gradient: float32 [256, 256], P('seqhi')
All inputs are finite; a program needn't handle non-finite values.
Results may differ from a plain program's by a relative error of at most 0.0062.
Values may be sent and summed in bfloat16 or wider, within the bound.
A program may use at most 64 MiB of HBM per device.

v0:
```python
import jax
import jax.numpy as jnp
from jax import lax
from jax.sharding import PartitionSpec as P


def passed_along(block, axis, distance):
    devices = range(lax.axis_size(axis))
    route = [(i - distance, i) for i in devices if i - distance in devices]
    return lax.ppermute(block, axis, route)


def pass_tap(block, steps):
    return passed_along(block, "seqhi", steps)


def layer_forward_step(layer_input, conv_weight, projection_weight, steps):
    earlier_samples = pass_tap(layer_input, steps)
    stacked_taps = jnp.concatenate([earlier_samples, layer_input], 1)
    gated_mixture = jnp.dot(stacked_taps, conv_weight, preferred_element_type=jnp.float32)
    half = conv_weight.shape[1] // 2
    hidden_state = (
        jnp.tanh(gated_mixture[:, :half]) * jax.nn.sigmoid(gated_mixture[:, half:])
    ).astype(jnp.bfloat16)
    output = (
        layer_input.astype(jnp.float32)
        + jnp.dot(hidden_state, projection_weight, preferred_element_type=jnp.float32)
    ).astype(jnp.bfloat16)
    return (output, stacked_taps, gated_mixture, hidden_state)


def layer_backward_step(
    output_cotangent,
    stacked_taps,
    gated_mixture,
    hidden_state,
    conv_weight,
    projection_weight,
    steps,
    gradient_scale,
):
    channel_width = output_cotangent.shape[1]
    half = conv_weight.shape[1] // 2
    dhid = lax.dot_general(
        output_cotangent,
        projection_weight,
        (((1,), (1,)), ((), ())),
        preferred_element_type=jnp.float32,
    )
    grad_outw = (
        lax.dot_general(
            hidden_state,
            output_cotangent,
            (((0,), (0,)), ((), ())),
            preferred_element_type=jnp.float32,
        )
        * gradient_scale
    )
    tanh_part = jnp.tanh(gated_mixture[:, :half])
    sig_part = jax.nn.sigmoid(gated_mixture[:, half:])
    dmixed = jnp.concatenate(
        [
            dhid * sig_part * (1.0 - tanh_part * tanh_part),
            dhid * tanh_part * sig_part * (1.0 - sig_part),
        ],
        1,
    ).astype(jnp.bfloat16)
    grad_filt = (
        lax.dot_general(
            stacked_taps, dmixed, (((0,), (0,)), ((), ())), preferred_element_type=jnp.float32
        )
        * gradient_scale
    )
    dstack = lax.dot_general(
        dmixed, conv_weight, (((1,), (1,)), ((), ())), preferred_element_type=jnp.float32
    )
    tap_position = dstack[:, :channel_width].astype(jnp.bfloat16)
    later_samples = pass_tap(tap_position, -steps)
    cot_prev = (
        output_cotangent.astype(jnp.float32)
        + dstack[:, channel_width:]
        + later_samples.astype(jnp.float32)
    ).astype(jnp.bfloat16)
    return (cot_prev, grad_filt, grad_outw)


def local(
    waveform_input,
    first_conv_weight,
    first_projection_weight,
    second_conv_weight,
    second_projection_weight,
    final_cotangent,
):
    total = waveform_input.shape[0] * lax.axis_size("seqlo") * lax.axis_size("seqhi")
    gradient_scale = jnp.float32(total) ** (-0.5)
    full_f1, full_o1, full_f2, full_o2 = (
        lax.all_gather(first_conv_weight, "seqhi", axis=0, tiled=True),
        lax.all_gather(first_projection_weight, "seqhi", axis=0, tiled=True),
        lax.all_gather(second_conv_weight, "seqhi", axis=0, tiled=True),
        lax.all_gather(second_projection_weight, "seqhi", axis=0, tiled=True),
    )
    second_layer_input, first_stacked_taps, first_gated_mixture, first_hidden_state = (
        layer_forward_step(waveform_input, full_f1, full_o1, 1)
    )
    ignored_value, second_stacked_taps, second_gated_mixture, second_hidden_state = (
        layer_forward_step(second_layer_input, full_f2, full_o2, 2)
    )
    middle_cotangent, g_f2, g_o2 = layer_backward_step(
        final_cotangent,
        second_stacked_taps,
        second_gated_mixture,
        second_hidden_state,
        full_f2,
        full_o2,
        2,
        gradient_scale,
    )
    input_cotangent, g_f1, g_o1 = layer_backward_step(
        middle_cotangent,
        first_stacked_taps,
        first_gated_mixture,
        first_hidden_state,
        full_f1,
        full_o1,
        1,
        gradient_scale,
    )
    summed = lax.psum((g_f1, g_o1, g_f2, g_o2), "seqlo")
    shares = (
        lax.psum_scatter(summed[0], "seqhi", scatter_dimension=0, tiled=True),
        lax.psum_scatter(summed[1], "seqhi", scatter_dimension=0, tiled=True),
        lax.psum_scatter(summed[2], "seqhi", scatter_dimension=0, tiled=True),
        lax.psum_scatter(summed[3], "seqhi", scatter_dimension=0, tiled=True),
    )
    return (input_cotangent, shares[0], shares[1], shares[2], shares[3])


def solution(mesh):
    placed = (
        P(("seqhi", "seqlo"), None),
        P("seqhi", None),
        P("seqhi", None),
        P("seqhi", None),
        P("seqhi", None),
        P(("seqhi", "seqlo"), None),
    )
    return jax.shard_map(
        local,
        mesh=mesh,
        in_specs=placed,
        out_specs=(
            P(("seqhi", "seqlo"), None),
            P("seqhi", None),
            P("seqhi", None),
            P("seqhi", None),
            P("seqhi", None),
        ),
        check_vma=False,
    )
```

profile of v0, /device:TPU:0, one launch (start us, length us, event | category | flops | bytes accessed | tf_op | source)
XLA Modules:
  0.0 281.0 jit_solution(5351742097442230568)
XLA Ops:
  7.2 3.5 %collective-permute-start = (bf16[2048,256]{1,0:T(8,128)(2,1)}, bf16[2048,256]{1,0:T(8,128)(2,1)}, u32[]{:S(2)}, u32[]{:S(2)}) collective-permute-start(bf16[2048,256]{1,0:T(8,128)(2,1)} %param.6), channel_id=1, source_target_pairs={{0,1},{1,2},{2,3},{4,5},{5,6},{6,7},{8,9},{9,10},{10,11},{12,13},{... | collective-permute-start | bytes 3145736 | tf_op jit(solution)/shard_map/ppermute | solution.py:10
  10.7 1.5 copy.11
  12.3 5.8 %all_gather.14 = bf16[256,256]{1,0:T(8,128)(2,1)S(1)} all-gather(bf16[64,256]{1,0:T(8,128)(2,1)S(1)} %copy-done.11), channel_id=1, replica_groups=mesh['seqlo'=8,'seqhi'=4] {'seqhi'}, dimensions={0}, use_global_device_ids=true | all-gather | bytes 163840 | tf_op jit(solution)/shard_map/all_gather | solution.py:99
  18.1 15.5 %all_gather.13 = bf16[512,512]{1,0:T(8,128)(2,1)S(1)} all-gather(bf16[128,512]{1,0:T(8,128)(2,1)S(1)} %copy-done.9), channel_id=1, replica_groups=mesh['seqlo'=8,'seqhi'=4] {'seqhi'}, dimensions={0}, use_global_device_ids=true | all-gather | bytes 655360 | tf_op jit(solution)/shard_map/all_gather | solution.py:98
  33.6 1.5 constant_dynamic-update-slice_fusion.1
  35.2 1.3 fusion.20
  39.0 3.4 %collective-permute-start.1 = (bf16[2048,256]{0,1:T(8,128)(2,1)S(1)}, bf16[2048,256]{0,1:T(8,128)(2,1)S(1)}, u32[]{:S(2)}, u32[]{:S(2)}) collective-permute-start(bf16[2048,256]{0,1:T(8,128)(2,1)S(1)} %fusion), channel_id=1, source_target_pairs={{0,2},{1,3},{4,6},{5,7},{8,10},{9,11},{12,14},{13,15},{16,18},{17,... | collective-permute-start | bytes 3145736 | tf_op jit(solution)/shard_map/ppermute | solution.py:10
  42.4 23.5 %all_gather.12 = bf16[256,256]{1,0:T(8,128)(2,1)S(1)} all-gather(bf16[64,256]{1,0:T(8,128)(2,1)S(1)} %copy-done.12), channel_id=1, replica_groups=mesh['seqlo'=8,'seqhi'=4] {'seqhi'}, dimensions={0}, use_global_device_ids=true | all-gather | bytes 163840 | tf_op jit(solution)/shard_map/all_gather | solution.py:101
  65.9 9.0 %all_gather.15 = bf16[512,512]{1,0:T(8,128)(2,1)S(1)} all-gather(bf16[128,512]{1,0:T(8,128)(2,1)S(1)} %copy-done.10), channel_id=1, replica_groups=mesh['seqlo'=8,'seqhi'=4] {'seqhi'}, dimensions={0}, use_global_device_ids=true | all-gather | bytes 655360 | tf_op jit(solution)/shard_map/all_gather | solution.py:100
  74.9 1.3 fusion.13
  76.5 1.3 multiply_convert_fusion.4
  77.9 1.3 fusion.12
  79.3 2.0 copy-done.5
  82.4 1.3 collective-permute-start.2
  83.7 1.7 convolution_multiply_fusion.2
  85.5 26.0 %collective-permute-done.2 = bf16[2048,256]{1,0:T(8,128)(2,1)} collective-permute-done((bf16[2048,256]{1,0:T(8,128)(2,1)}, bf16[2048,256]{1,0:T(8,128)(2,1)}, u32[]{:S(2)}, u32[]{:S(2)}) %collective-permute-start.2) | collective-permute-done | bytes 1048608 | tf_op jit(solution)/shard_map/ppermute | solution.py:10
  111.4 2.5 fusion.4
  115.1 4.5 %convolution_multiply_fusion = f32[512,512]{1,0:T(8,128)} fusion(bf16[2048,256]{0,1:T(8,128)(2,1)} %copy-done.15, bf16[2048,256]{0,1:T(8,128)(2,1)} %copy-done.14, bf16[2048,256]{0,1:T(8,128)(2,1)} %copy-done.8, bf16[2048,256]{0,1:T(8,128)(2,1)} %copy-done.13), kind=kOutput, calls=%fused_computation.29 | convolution fusion | flops 1082392576 | bytes 5242880 | tf_op jit(solution)/shard_map/dot_general | solution.py:69
  119.9 3.6 %multiply_convert_fusion.2 = (bf16[2048,256]{0,1:T(8,128)(2,1)S(1)}, bf16[2048,256]{0,1:T(8,128)(2,1)S(1)}) fusion(f32[2048,512]{0,1:T(8,128)} %copy-done, bf16[2048,256]{1,0:T(8,128)(2,1)S(1)} %fusion.4, bf16[256,256]{1,0:T(8,128)(2,1)S(1)} %all_gather.14), kind=kOutput, calls=%fused_computation.25 | convolution fusion | flops 275251200 | bytes 7471104 | tf_op jit(solution)/shard_map/dot_general | solution.py:44
  124.8 2.3 convolution_multiply_fusion.1
  127.1 3.0 %fusion.11 = f32[2048,512]{1,0:T(8,128)S(1)} fusion(bf16[512,512]{1,0:T(8,128)(2,1)} %copy-done.6, bf16[2048,256]{0,1:T(8,128)(2,1)} %copy-done.17, bf16[2048,256]{0,1:T(8,128)(2,1)} %copy-done.16), kind=kOutput, calls=%fused_computation.31 | convolution fusion | flops 1077936128 | bytes 6815744 | tf_op jit(solution)/shard_map/dot_general | solution.py:74
  130.1 1.9 copy-done.4
  132.2 1.3 collective-permute-start.3
  133.5 2.1 reduce-scatter.7.cloned.1.call-done
  135.6 27.5 %reduce-scatter.9.cloned.1.call-done = f32[128,512]{1,0:T(8,128)} async-done(((f32[512,512]{1,0:T(8,128)}), f32[128,512]{1,0:T(8,128)}) %reduce-scatter.9.cloned.1.call-update) | async-done | bytes 262160 | tf_op jit(solution)/shard_map/reduce_scatter | solution.py:133
  163.1 27.5 %reduce-scatter.5.cloned.1.call-done = f32[128,512]{1,0:T(8,128)} async-done(((f32[512,512]{1,0:T(8,128)}), f32[128,512]{1,0:T(8,128)}) %reduce-scatter.5.cloned.1.call-update) | async-done | bytes 262160 | tf_op jit(solution)/shard_map/reduce_scatter | solution.py:131
  190.5 2.9 %fusion.2 = bf16[2048,256]{1,0:T(8,128)(2,1)} fusion(f32[2048,512]{1,0:T(8,128)} %copy-done.4, bf16[2048,256]{1,0:T(8,128)(2,1)S(1)} %collective-permute-done.3, bf16[2048,256]{1,0:T(8,128)(2,1)S(1)} %fusion.4), kind=kLoop, calls=%fused_computation.5 | loop fusion | flops 2621440 | bytes 5242880 | tf_op jit(solution)/shard_map/convert_element_type | solution.py:83
  193.4 74.8 %all-reduce.3.cloned.1.call-done = (f32[128,512]{1,0:T(8,128)}, f32[64,256]{1,0:T(8,128)}, f32[128,512]{1,0:T(8,128)}, f32[64,256]{1,0:T(8,128)}) async-done(((f32[128,512]{1,0:T(8,128)}, f32[64,256]{1,0:T(8,128)}, f32[128,512]{1,0:T(8,128)}, f32[64,256]{1,0:T(8,128)}), (f32[128,512]{1,0:T(8,128)}, f32[64,256]{1,0:T(8,128)}, f32[128,512]{1,0:T(8,128)}, f32[64,256]{1,0:T(8,128)})) %all-reduce.3.cloned.1.call-update) | async-done | bytes 655376 | tf_op jit(solution)/shard_map/psum | solution.py:129
  268.2 1.7 copy.17
  269.9 1.5 copy.18
  271.3 1.7 copy.19
  273.0 1.5 copy.20
  (54 shorter events, 7.1 us)
Async XLA Ops:
  7.2 5.1 %copy-start.11 = (bf16[64,256]{1,0:T(8,128)(2,1)S(1)}, bf16[64,256]{1,0:T(8,128)(2,1)}, u32[]{:S(2)}) copy-start(bf16[64,256]{1,0:T(8,128)(2,1)} %param.8) | copy-start | bytes 98308
  7.2 10.9 %copy-start.9 = (bf16[128,512]{1,0:T(8,128)(2,1)S(1)}, bf16[128,512]{1,0:T(8,128)(2,1)}, u32[]{:S(2)}) copy-start(bf16[128,512]{1,0:T(8,128)(2,1)} %param.7) | copy-start | bytes 393220
  7.2 126.3 %reduce-scatter.11.cloned.1.call-start = ((), (), s32[]{:S(2)}) async-start(), calls=%async_computation.7 | async-start | bytes 327680 | tf_op jit(solution)/shard_map/reduce_scatter | solution.py:134
  7.2 26.4 %collective-permute-start = (bf16[2048,256]{1,0:T(8,128)(2,1)}, bf16[2048,256]{1,0:T(8,128)(2,1)}, u32[]{:S(2)}, u32[]{:S(2)}) collective-permute-start(bf16[2048,256]{1,0:T(8,128)(2,1)} %param.6), channel_id=1, source_target_pairs={{0,1},{1,2},{2,3},{4,5},{5,6},{6,7},{8,9},{9,10},{10,11},{12,13},{... | collective-permute-start | bytes 3145736 | tf_op jit(solution)/shard_map/ppermute | solution.py:10
  12.2 22.8 %copy-start.3 = (bf16[2048,256]{1,0:T(8,128)(2,1)S(1)}, bf16[2048,256]{1,0:T(8,128)(2,1)}, u32[]{:S(2)}) copy-start(bf16[2048,256]{1,0:T(8,128)(2,1)} %param.6) | copy-start | bytes 3145732
  33.6 1.6 copy-start.6
  36.5 1.9 copy-start
  38.5 37.8 %copy-start.1 = (bf16[2048,256]{0,1:T(8,128)(2,1)}, bf16[2048,256]{0,1:T(8,128)(2,1)S(1)}, u32[]{:S(2)}) copy-start(bf16[2048,256]{0,1:T(8,128)(2,1)S(1)} %multiply_convert_fusion.5) | copy-start | bytes 3145732
  38.5 3.9 %copy-start.12 = (bf16[64,256]{1,0:T(8,128)(2,1)S(1)}, bf16[64,256]{1,0:T(8,128)(2,1)}, u32[]{:S(2)}) copy-start(bf16[64,256]{1,0:T(8,128)(2,1)} %param.10) | copy-start | bytes 98308
  38.5 27.5 %copy-start.10 = (bf16[128,512]{1,0:T(8,128)(2,1)S(1)}, bf16[128,512]{1,0:T(8,128)(2,1)}, u32[]{:S(2)}) copy-start(bf16[128,512]{1,0:T(8,128)(2,1)} %param.9) | copy-start | bytes 393220
  39.0 37.3 %copy-start.8 = (bf16[2048,256]{0,1:T(8,128)(2,1)}, bf16[2048,256]{0,1:T(8,128)(2,1)S(1)}, u32[]{:S(2)}) copy-start(bf16[2048,256]{0,1:T(8,128)(2,1)S(1)} %fusion) | copy-start | bytes 3145732
  39.0 35.9 %collective-permute-start.1 = (bf16[2048,256]{0,1:T(8,128)(2,1)S(1)}, bf16[2048,256]{0,1:T(8,128)(2,1)S(1)}, u32[]{:S(2)}, u32[]{:S(2)}) collective-permute-start(bf16[2048,256]{0,1:T(8,128)(2,1)S(1)} %fusion), channel_id=1, source_target_pairs={{0,2},{1,3},{4,6},{5,7},{8,10},{9,11},{12,14},{13,15},{16,18},{17,... | collective-permute-start | bytes 3145736 | tf_op jit(solution)/shard_map/ppermute | solution.py:10
  74.9 1.6 copy-start.7
  74.9 1.3 copy-start.13
  77.8 1.3 copy-start.14
  77.9 1.4 copy-start.15
  79.3 2.0 copy-start.5
  82.4 29.0 %collective-permute-start.2 = (bf16[2048,256]{1,0:T(8,128)(2,1)}, bf16[2048,256]{1,0:T(8,128)(2,1)}, u32[]{:S(2)}, u32[]{:S(2)}) collective-permute-start(bf16[2048,256]{1,0:T(8,128)(2,1)} %slice.101), channel_id=1, source_target_pairs={{2,0},{3,1},{6,4},{7,5},{10,8},{11,9},{14,12},{15,13},{18,16},{19,... | collective-permute-start | bytes 3145736 | tf_op jit(solution)/shard_map/ppermute | solution.py:10
  85.4 50.2 %reduce-scatter.7.cloned.1.call-start = ((), (), s32[]{:S(2)}) async-start(), calls=%async_computation.5 | async-start | bytes 327680 | tf_op jit(solution)/shard_map/reduce_scatter | solution.py:132
  85.4 28.5 %copy-start.2 = (bf16[2048,256]{0,1:T(8,128)(2,1)S(1)}, bf16[2048,256]{0,1:T(8,128)(2,1)}, u32[]{:S(2)}) copy-start(bf16[2048,256]{0,1:T(8,128)(2,1)} %copy-done.1) | copy-start | bytes 3145732
  115.1 48.0 %reduce-scatter.9.cloned.1.call-start = ((), (), s32[]{:S(2)}) async-start(), calls=%async_computation.6 | async-start | bytes 1310720 | tf_op jit(solution)/shard_map/reduce_scatter | solution.py:133
  119.6 70.9 %reduce-scatter.5.cloned.1.call-start = ((), (), s32[]{:S(2)}) async-start(), calls=%async_computation.4 | async-start | bytes 1310720 | tf_op jit(solution)/shard_map/reduce_scatter | solution.py:131
  123.4 1.0 copy-start.16
  123.4 1.3 copy-start.17
  127.0 141.1 %all-reduce.3.cloned.1.call-start = ((), (), s32[]{:S(2)}) async-start(), calls=%async_computation.8 | async-start | bytes 1310720 | tf_op jit(solution)/shard_map/psum | solution.py:129
  130.1 1.9 copy-start.4
  132.2 58.4 %collective-permute-start.3 = (bf16[2048,256]{1,0:T(8,128)(2,1)S(1)}, bf16[2048,256]{1,0:T(8,128)(2,1)S(1)}, u32[]{:S(2)}, u32[]{:S(2)}) collective-permute-start(bf16[2048,256]{1,0:T(8,128)(2,1)S(1)} %slice.100), channel_id=1, source_target_pairs={{1,0},{2,1},{3,2},{5,4},{6,5},{7,6},{9,8},{10,9},{11,10},{13,12},{... | collective-permute-start | bytes 3145736 | tf_op jit(solution)/shard_map/ppermute | solution.py:10
Sparse Core Ops, SparseCore 0:
  85.5 24.8 reduce-scatter.10
  115.2 20.3 reduce-scatter.6
  138.1 24.8 reduce-scatter.8
  165.6 24.8 reduce-scatter.4
  194.1 74.0 all-reduce.2
where the time goes:
time: 282 us; the launch traced here: 281 us
  waiting for transfers between devices  158 us (56%)
  blocking collectives  53.8 us (19%)
  matrix products  21.9 us (8%)
  local copies, waits for them, and re-layouts  17.3 us (6%)
  between operations  14.1 us (5%)
  starting transfers between devices  9.87 us (3%)
  other arithmetic  6.17 us (2%)
    psum x1, waiting for transfers between devices, local(): summed = lax.psum((g_f1, g_o1, g_f2, g_o2), 'seqlo')  74.8 us
    reduce_scatter x1, waiting for transfers between devices, local(): lax.psum_scatter(summed[2], 'seqhi', scatter_dimension=0, tiled=True)  27.5 us
    reduce_scatter x1, waiting for transfers between devices, local(): lax.psum_scatter(summed[0], 'seqhi', scatter_dimension=0, tiled=True)  27.5 us
    ppermute x4, waiting for transfers between devices, passed_along(): return lax.ppermute(block, axis, route)  26 us
    all_gather x1, blocking collectives, local(): lax.all_gather(second_projection_weight, 'seqhi', axis=0, tiled=True)  23.5 us
    unnamed x42, local copies, waits for them, and re-layouts  16 us
    all_gather x1, blocking collectives, local(): lax.all_gather(first_conv_weight, 'seqhi', axis=0, tiled=True)  15.5 us
    ppermute x4, starting transfers between devices, passed_along(): return lax.ppermute(block, axis, route)  9.49 us
  transfers between devices with their start and end apart: 9, of which 5 were waited for; matrix products, arithmetic and copies ran while one was open for 8% of the time, Pallas kernels for 0%

commit v1 on v0

v1 whole, which is shorter than its diff:
```python
import functools

import jax
import jax.numpy as jnp
from jax import lax
from jax.experimental import pallas as pl
from jax.experimental.pallas import tpu as pltpu
from jax.sharding import PartitionSpec as P

F32, BF16 = jnp.float32, jnp.bfloat16
MESH = pl.DeviceIdType.MESH


def flip(index, bits):
    b = 1
    while b <= bits:
        if bits & b:
            index = index + b - 2 * b * lax.rem(lax.div(index, b), 2)
        b *= 2
    return index


def dot(a, b):
    return jnp.dot(a, b, preferred_element_type=F32)


def dot_rows(a, b):
    return lax.dot_general(a, b, (((0,), (0,)), ((), ())), preferred_element_type=F32)


def dot_cols(a, b):
    return lax.dot_general(a, b, (((1,), (1,)), ((), ())), preferred_element_type=F32)


def sigmoid(v):
    return 0.5 * jnp.tanh(0.5 * v) + 0.5


def kernel(
    nhi, nlo, chunks, scale,
    x_in, f1_in, p1_in, f2_in, p2_in, c_in,
    y_out, gf1_out, gp1_out, gf2_out, gp2_out,
    wf1, wp1, wf2, wp2, xs, cs, ys, t1, s1, h1, c1,
    gf1, gp1, gf2, gp2, g32, gb, rb, lb, lr, ag,
    w_send, w_recv, w_own, x_send, x_recv, c_send, c_recv, y_send, y_recv, own,
    h_send, h_recv, l_send, l_recv, a_send, a_recv,
):
    hi, lo = lax.axis_index("seqhi"), lax.axis_index("seqlo")
    m, width = xs.shape[1], xs.shape[2]
    mc = m // chunks
    half = width
    r, rp = f1_in.shape[0], p1_in.shape[0]
    fcols, pcols = f1_in.shape[1] // 128, p1_in.shape[1] // 128
    length = g32.shape[2]
    piece = lr.shape[2]

    def remote(src, dst, send, recv, axis, partner):
        return pltpu.make_async_remote_copy(
            src_ref=src, dst_ref=dst, send_sem=send, recv_sem=recv,
            device_id={axis: partner}, device_id_type=MESH,
        )

    barrier = pltpu.get_barrier_semaphore()
    for j in range(1, nhi):
        pl.semaphore_signal(barrier, inc=1, device_id={"seqhi": flip(hi, j)}, device_id_type=MESH)
    for j in range(1, nlo):
        pl.semaphore_signal(barrier, inc=1, device_id={"seqlo": flip(lo, j)}, device_id_type=MESH)

    inputs = (f1_in, p1_in, f2_in, p2_in)
    full = (wf1, wp1, wf2, wp2)
    local_copies = []
    for a in range(4):
        size = inputs[a].shape[0]
        here = pl.ds(pl.multiple_of(hi * size, size), size)
        local_copies.append(pltpu.make_async_copy(inputs[a], full[a].at[here], w_own.at[a]))
    mine = pl.ds(pl.multiple_of(hi * m, m), m)
    local_copies.append(pltpu.make_async_copy(x_in.at[mine], xs.at[hi], w_own.at[4]))
    local_copies.append(pltpu.make_async_copy(c_in.at[mine], cs.at[hi], w_own.at[5]))
    for copy in local_copies:
        copy.start()

    pl.semaphore_wait(barrier, nhi - 1 + nlo - 1)

    bits = []
    b = nhi // 2
    while b >= 1:
        bits.append(b)
        b //= 2
    plan = []
    held = [0]
    for b in bits:
        for h in held:
            plan.append((h, b))
        held = held + [h ^ b for h in held]

    def weight_copy(a, at):
        h, b = plan[at]
        size = inputs[a].shape[0]
        there = pl.ds(pl.multiple_of(flip(hi, h) * size, size), size)
        src = inputs[a] if h == 0 else full[a].at[there]
        return remote(src, full[a].at[there], w_send.at[a, at], w_recv.at[a, at], "seqhi", flip(hi, b))

    def sample_copy(src, dst, send, recv, j, k):
        partner = flip(hi, j)
        start = pl.multiple_of(partner * m + k * mc, mc)
        part = pl.ds(pl.multiple_of(k * mc, mc), mc)
        return remote(src.at[pl.ds(start, mc)], dst.at[hi, part], send.at[j, k], recv.at[j, k], "seqhi", partner)

    def x_copy(j, k):
        return sample_copy(x_in, xs, x_send, x_recv, j, k)

    def c_copy(j, k):
        return sample_copy(c_in, cs, c_send, c_recv, j, k)

    for a in range(4):
        for at in range(len(plan)):
            if plan[at][0] == 0:
                weight_copy(a, at).start()
    for k in range(chunks):
        for j in range(nhi - 1, 0, -1):
            x_copy(j, k).start()
        for j in range(nhi - 1, 0, -1):
            c_copy(j, k).start()

    for ref in (gf1, gp1, gf2, gp2):
        ref[...] = jnp.zeros_like(ref)
    if length > r * fcols + rp * pcols:
        g32[...] = jnp.zeros_like(g32)
        gb[...] = jnp.zeros_like(gb)

    for copy in local_copies:
        copy.wait()
    arrived = {h ^ b: at for at, (h, b) in enumerate(plan)}
    for a in range(4):
        waited = set()
        for at, (h, b) in enumerate(plan):
            if h:
                if arrived[h] not in waited:
                    weight_copy(a, arrived[h]).wait_recv()
                    waited.add(arrived[h])
                weight_copy(a, at).start()
        for at in range(len(plan)):
            if at not in waited:
                weight_copy(a, at).wait_recv()

    def gates(mixed):
        return jnp.tanh(mixed[:, :half]), sigmoid(mixed[:, half:])

    def mix(v, weight, steps):
        cut = steps * mc
        current = dot(v, weight[width:, :])
        delayed = dot(v[:-cut], weight[:width, :])
        return jnp.concatenate([current[:cut], current[cut:] + delayed], 0)

    def back(v, c, t, s, hidden, weight, projection, gf, gp, steps):
        cut = steps * mc
        dhid = dot_cols(c, projection[...])
        gp[...] += dot_rows(hidden, c)
        dmixed = jnp.concatenate(
            [dhid * s * (1.0 - t * t), dhid * t * s * (1.0 - s)], 1
        ).astype(BF16)
        gf[width:, :] += dot_rows(v, dmixed)
        gf[:width, :] += dot_rows(v[:-cut], dmixed[cut:])
        current = c.astype(F32) + dot_cols(dmixed, weight[width:, :])
        tap = dot_cols(dmixed[cut:], weight[:width, :]).astype(BF16).astype(F32)
        return jnp.concatenate([current[:-cut] + tap, current[-cut:]], 0).astype(BF16)

    rows = nhi * mc

    def first_loop(k, carry):
        part = pl.ds(pl.multiple_of(k * mc, mc), mc)
        for j in range(1, nhi):
            x_copy(j, k).wait_recv()
        x = xs[:, part, :].reshape(rows, width)
        t, s = gates(mix(x, wf1, 1))
        hidden = (t * s).astype(BF16)
        t1[k], s1[k], h1[k] = t, s, hidden
        x2 = (x.astype(F32) + dot(hidden, wp1[...])).astype(BF16)
        t, s = gates(mix(x2, wf2, 2))
        hidden = (t * s).astype(BF16)
        for j in range(1, nhi):
            c_copy(j, k).wait_recv()
        c = cs[:, part, :].reshape(rows, width)
        c1[k] = back(x2, c, t, s, hidden, wf2, wp2, gf2, gp2, 2)
        return carry

    lax.fori_loop(0, chunks, first_loop, 0)

    def pack(layer):
        gf, gp = (gf1, gp1) if layer == 0 else (gf2, gp2)
        for j in range(nhi):
            q = flip(hi, j)
            f_rows = pl.ds(pl.multiple_of(q * r, r), r)
            p_rows = pl.ds(pl.multiple_of(q * rp, rp), rp)
            for i in range(fcols + pcols):
                if i < fcols:
                    values = gf[f_rows, i * 128:(i + 1) * 128]
                    at = slice(i * r, (i + 1) * r)
                else:
                    col = i - fcols
                    values = gp[p_rows, col * 128:(col + 1) * 128]
                    at = slice(fcols * r + col * rp, fcols * r + (col + 1) * rp)
                if j & 1:
                    gb[layer, j, at, :] = values.astype(BF16)
                else:
                    g32[layer, j, at, :] = values

    def hi_copy(layer, j):
        b = j & -j
        return remote(
            gb.at[layer, j], rb.at[layer, j], h_send.at[layer, j], h_recv.at[layer, j],
            "seqhi", flip(hi, b),
        )

    def hi_slots(s):
        return [j for j in range(nhi) if j & -j == 1 << s]

    def hi_start(layer, s):
        for j in hi_slots(s):
            hi_copy(layer, j).start()

    def hi_finish(layer, s):
        for j in hi_slots(s):
            hi_copy(layer, j).wait_recv()
            target = j ^ (1 << s)
            total = g32[layer, target] + rb[layer, j].astype(F32)
            g32[layer, target] = total
            if target and target & -target == 2 << s:
                gb[layer, target] = total.astype(BF16)

    def piece_at(index):
        return pl.ds(pl.multiple_of(index * piece, piece), piece)

    def lo_copy(layer, j):
        partner = flip(lo, j)
        return remote(
            lb.at[layer, piece_at(partner)], lr.at[layer, j], l_send.at[layer, j],
            l_recv.at[layer, j], "seqlo", partner,
        )

    def lo_start(layer):
        lb[layer] = g32[layer, 0].astype(BF16)
        for j in range(nlo - 1, 0, -1):
            lo_copy(layer, j).start()

    def ag_copy(layer, j):
        return remote(
            ag.at[layer, piece_at(lo)], ag.at[layer, piece_at(lo)], a_send.at[layer, j],
            a_recv.at[layer, j], "seqlo", flip(lo, j),
        )

    def lo_finish(layer):
        total = g32[layer, 0, piece_at(lo), :]
        for j in range(1, nlo):
            lo_copy(layer, j).wait_recv()
            total = total + lr[layer, j].astype(F32)
        ag[layer, piece_at(lo), :] = (total * scale).astype(BF16)
        for j in range(nlo - 1, 0, -1):
            ag_copy(layer, j).start()

    def ag_finish(layer):
        gf, gp = (gf1_out, gp1_out) if layer == 0 else (gf2_out, gp2_out)
        for j in range(1, nlo):
            ag_copy(layer, j).wait_recv()
        for i in range(fcols):
            gf[:, i * 128:(i + 1) * 128] = ag[layer, i * r:(i + 1) * r, :].astype(F32)
        for i in range(pcols):
            at = fcols * r + i * rp
            gp[:, i * 128:(i + 1) * 128] = ag[layer, at:at + rp, :].astype(F32)

    stages = len(bits)

    def phases(layer):
        steps = []
        for s in range(stages):
            def step(s=s):
                hi_finish(layer, s)
                if s + 1 < stages:
                    hi_start(layer, s + 1)
                else:
                    lo_start(layer)
            steps.append(step)
        steps.append(lambda: lo_finish(layer))
        return steps

    def y_copy(j, k):
        partner = flip(hi, j)
        start = pl.multiple_of(hi * m + k * mc, mc)
        part = pl.ds(pl.multiple_of(k * mc, mc), mc)
        return remote(
            ys.at[partner, part], y_out.at[pl.ds(start, mc)], y_send.at[j, k], y_recv.at[j, k],
            "seqhi", partner,
        )

    def y_local(k):
        start = pl.multiple_of(hi * m + k * mc, mc)
        part = pl.ds(pl.multiple_of(k * mc, mc), mc)
        return pltpu.make_async_copy(ys.at[hi, part], y_out.at[pl.ds(start, mc)], own.at[k])

    pack(1)
    hi_start(1, 0)
    second = phases(1)

    def second_loop(k, carry):
        part = pl.ds(pl.multiple_of(k * mc, mc), mc)
        x = xs[:, part, :].reshape(rows, width)
        y = back(x, c1[k], t1[k], s1[k], h1[k], wf1, wp1, gf1, gp1, 1)
        ys[:, part, :] = y.reshape(nhi, mc, width)
        for j in range(nhi - 1, 0, -1):
            y_copy(j, k).start()
        y_local(k).start()
        for i in range(min(len(second), chunks)):
            pl.when(k == i)(second[i])
        return carry

    lax.fori_loop(0, chunks, second_loop, 0)

    pack(0)
    hi_start(0, 0)
    for step in second[chunks:]:
        step()
    for step in phases(0):
        step()
    ag_finish(1)
    ag_finish(0)

    for a in range(4):
        for at in range(len(plan)):
            weight_copy(a, at).wait_send()
    for k in range(chunks):
        for j in range(1, nhi):
            x_copy(j, k).wait_send()
            c_copy(j, k).wait_send()
            y_copy(j, k).wait()
        y_local(k).wait()
    for layer in range(2):
        for j in range(1, nhi):
            hi_copy(layer, j).wait_send()
        for j in range(1, nlo):
            lo_copy(layer, j).wait_send()
            ag_copy(layer, j).wait_send()


def local(x, f1, p1, f2, p2, c):
    nhi, nlo = lax.axis_size("seqhi"), lax.axis_size("seqlo")
    samples, width = x.shape
    chunks = 4
    m = samples // nhi
    mc = m // chunks
    scale = float(samples * nhi * nlo) ** -0.5
    r, h = f1.shape
    rp = p1.shape[0]
    need = r * (h // 128) + rp * (width // 128)
    piece = -(-need // (16 * nlo)) * 16
    length = piece * nlo
    rows = nhi * mc
    dma = pltpu.SemaphoreType.DMA
    any_spec = pl.BlockSpec(memory_space=pl.ANY)
    vmem = pl.BlockSpec(memory_space=pltpu.VMEM)
    shape = jax.ShapeDtypeStruct
    return pl.pallas_call(
        functools.partial(kernel, nhi, nlo, chunks, scale),
        out_shape=(
            shape(x.shape, BF16), shape(f1.shape, F32), shape(p1.shape, F32),
            shape(f2.shape, F32), shape(p2.shape, F32),
        ),
        in_specs=[any_spec] * 6,
        out_specs=(any_spec, vmem, vmem, vmem, vmem),
        scratch_shapes=[
            pltpu.VMEM((r * nhi, h), BF16),
            pltpu.VMEM((rp * nhi, width), BF16),
            pltpu.VMEM((r * nhi, h), BF16),
            pltpu.VMEM((rp * nhi, width), BF16),
            pltpu.VMEM((nhi, m, width), BF16),
            pltpu.VMEM((nhi, m, width), BF16),
            pltpu.VMEM((nhi, m, width), BF16),
            pltpu.VMEM((chunks, rows, h // 2), F32),
            pltpu.VMEM((chunks, rows, h // 2), F32),
            pltpu.VMEM((chunks, rows, h // 2), BF16),
            pltpu.VMEM((chunks, rows, width), BF16),
            pltpu.VMEM((r * nhi, h), F32),
            pltpu.VMEM((rp * nhi, width), F32),
            pltpu.VMEM((r * nhi, h), F32),
            pltpu.VMEM((rp * nhi, width), F32),
            pltpu.VMEM((2, nhi, length, 128), F32),
            pltpu.VMEM((2, nhi, length, 128), BF16),
            pltpu.VMEM((2, nhi, length, 128), BF16),
            pltpu.VMEM((2, length, 128), BF16),
            pltpu.VMEM((2, nlo, piece, 128), BF16),
            pltpu.VMEM((2, length, 128), BF16),
            dma((4, nhi)), dma((4, nhi)), dma((6,)),
            dma((nhi, chunks)), dma((nhi, chunks)),
            dma((nhi, chunks)), dma((nhi, chunks)),
            dma((nhi, chunks)), dma((nhi, chunks)), dma((chunks,)),
            dma((2, nhi)), dma((2, nhi)),
            dma((2, nlo)), dma((2, nlo)),
            dma((2, nlo)), dma((2, nlo)),
        ],
        compiler_params=pltpu.CompilerParams(
            collective_id=0, has_side_effects=True, vmem_limit_bytes=48 * 1024 * 1024
        ),
        cost_estimate=pl.CostEstimate(
            flops=16 * samples * width * h * 2, bytes_accessed=8 * samples * width,
            transcendentals=4 * samples * h,
        ),
    )(x, f1, p1, f2, p2, c)


def solution(mesh):
    rows = P(("seqhi", "seqlo"), None)
    weights = P("seqhi", None)
    return jax.shard_map(
        local,
        mesh=mesh,
        in_specs=(rows, weights, weights, weights, weights, rows),
        out_specs=(rows, weights, weights, weights, weights),
        check_vma=False,
    )
```

time: 282 us -> 84.3 us (0.30)
  waiting for transfers between devices: 158 us -> 0 us
  Pallas kernels: 0 us -> 73.9 us
  blocking collectives: 53.8 us -> 0 us
  matrix products: 21.9 us -> 0 us
  between operations: 14.1 us -> 0.66 us
  starting transfers between devices: 9.87 us -> 0 us
  local copies, waits for them, and re-layouts: 17.3 us -> 9.4 us
  other arithmetic: 6.17 us -> 0 us
    psum x1 -> x0, waiting for transfers between devices: 74.8 us -> none  [local(): summed = lax.psum((g_f1, g_o1, g_f2, g_o2), 'seqlo')]
    pallas_call x0 -> x1, Pallas kernels: none -> 73.9 us  [local(): pl.pallas_call(functools.partial(kernel, nhi, nlo, chunks, scale), out_sh...]
    reduce_scatter x4 -> x0, waiting for transfers between devices: 57 us -> none  [the longest x1 27.5 us: local(): lax.psum_scatter(summed[2], 'seqhi', scatter_dimension=0, tiled=True)]
    all_gather x4 -> x0, blocking collectives: 53.8 us -> none  [the longest x1 23.5 us: local(): lax.all_gather(second_projection_weight, 'seqhi', axis=0, tiled=True)]
    ppermute x4 -> x0, waiting for transfers between devices: 26 us -> none  [passed_along(): return lax.ppermute(block, axis, route)]
    dot_general x11 -> x0, matrix products: 21.9 us -> none  [the longest x2 6.73 us: layer_backward_step(): lax.dot_general(stacked_taps, dmixed, (((0,), (0,)), ((), ())), preferred...]
    ppermute x4 -> x0, starting transfers between devices: 9.49 us -> none  [passed_along(): return lax.ppermute(block, axis, route)]
    unnamed x42 -> x17, local copies, waits for them, and re-layouts: 16 us -> 9.4 us
  transfers between devices with their start and end apart: 9 -> 0, of which waited for: 5 -> 0; matrix products, arithmetic and copies ran while one was open for 8% -> 0% of each run, Pallas kernels for 0% -> 0%
where the time goes in v1:
time: 84.3 us; the launch traced here: 83.9 us
  Pallas kernels  73.9 us (88%)
  local copies, waits for them, and re-layouts  9.4 us (11%)
    pallas_call x1, Pallas kernels, local(): pl.pallas_call(functools.partial(kernel, nhi, nlo, chunks, scale), out_sh...  73.9 us
    unnamed x17, local copies, waits for them, and re-layouts  9.4 us

profile of v1, /device:TPU:0, one launch (start us, length us, event | category | flops | bytes accessed | tf_op | source)
XLA Modules:
  0.0 83.9 jit_solution(10797935975598873172)
XLA Ops:
  0.6 0.0 copy-start
  0.6 1.2 %copy-done = bf16[2048,256]{1,0:T(8,128)(2,1)S(1)} copy-done((bf16[2048,256]{1,0:T(8,128)(2,1)S(1)}, bf16[2048,256]{1,0:T(8,128)(2,1)}, u32[]{:S(2)}) %copy-start) | copy-done | bytes 1048600
  1.9 0.0 copy-start.1
  1.9 1.2 %copy-done.1 = bf16[2048,256]{1,0:T(8,128)(2,1)S(1)} copy-done((bf16[2048,256]{1,0:T(8,128)(2,1)S(1)}, bf16[2048,256]{1,0:T(8,128)(2,1)}, u32[]{:S(2)}) %copy-start.1) | copy-done | bytes 1048600
  3.1 0.0 copy-start.2
  3.1 0.9 %copy-done.2 = bf16[128,512]{1,0:T(8,128)(2,1)S(1)} copy-done((bf16[128,512]{1,0:T(8,128)(2,1)S(1)}, bf16[128,512]{1,0:T(8,128)(2,1)}, u32[]{:S(2)}) %copy-start.2) | copy-done | bytes 131096
  4.0 0.0 copy-start.3
  4.0 0.9 %copy-done.3 = bf16[128,512]{1,0:T(8,128)(2,1)S(1)} copy-done((bf16[128,512]{1,0:T(8,128)(2,1)S(1)}, bf16[128,512]{1,0:T(8,128)(2,1)}, u32[]{:S(2)}) %copy-start.3) | copy-done | bytes 131096
  4.9 0.0 copy-start.4
  4.9 0.8 copy-done.4
  5.7 0.0 copy-start.5
  5.7 0.8 copy-done.5
  6.4 73.9 %shard_map.101 = (bf16[2048,256]{1,0:T(8,128)(2,1)S(1)}, f32[128,512]{1,0:T(8,128)S(1)}, f32[64,256]{1,0:T(8,128)S(1)}, f32[128,512]{1,0:T(8,128)S(1)}, f32[64,256]{1,0:T(8,128)S(1)}) custom-call(bf16[2048,256]{1,0:T(8,128)(2,1)S(1)} %copy-done, bf16[128,512]{1,0:T(8,128)(2,1)S(1)} %copy-done.2, bf16[64,256]{1,0:T(8,128)(2,1)S(1)} %copy-done.4, ...), custom_call_target="tpu_custom_call" | custom-call | flops 8589934592 | bytes 4194304 | tf_op jit(solution)/shard_map/pallas_call | solution.py:361
  80.3 1.0 %copy.16 = bf16[2048,256]{1,0:T(8,128)(2,1)} copy(bf16[2048,256]{1,0:T(8,128)(2,1)S(1)} %get-tuple-element.10) | data formatting | bytes 2097152
  81.3 0.7 copy.17
  82.0 0.6 copy.18
  82.6 0.7 copy.19
  83.3 0.6 copy.20
Async XLA Ops:
  0.6 1.2 %copy-start = (bf16[2048,256]{1,0:T(8,128)(2,1)S(1)}, bf16[2048,256]{1,0:T(8,128)(2,1)}, u32[]{:S(2)}) copy-start(bf16[2048,256]{1,0:T(8,128)(2,1)} %x_in.1) | copy-start | bytes 3145732
  1.9 1.2 %copy-start.1 = (bf16[2048,256]{1,0:T(8,128)(2,1)S(1)}, bf16[2048,256]{1,0:T(8,128)(2,1)}, u32[]{:S(2)}) copy-start(bf16[2048,256]{1,0:T(8,128)(2,1)} %c_in.1) | copy-start | bytes 3145732
  3.1 0.9 %copy-start.2 = (bf16[128,512]{1,0:T(8,128)(2,1)S(1)}, bf16[128,512]{1,0:T(8,128)(2,1)}, u32[]{:S(2)}) copy-start(bf16[128,512]{1,0:T(8,128)(2,1)} %f1_in.1) | copy-start | bytes 393220
  4.0 0.9 %copy-start.3 = (bf16[128,512]{1,0:T(8,128)(2,1)S(1)}, bf16[128,512]{1,0:T(8,128)(2,1)}, u32[]{:S(2)}) copy-start(bf16[128,512]{1,0:T(8,128)(2,1)} %f2_in.1) | copy-start | bytes 393220
  4.9 0.8 copy-start.4
  5.7 0.8 copy-start.5

commit v2 on v1

--- a/solution.py
+++ b/solution.py
@@ -40,7 +40,7 @@
     nhi, nlo, chunks, scale,
     x_in, f1_in, p1_in, f2_in, p2_in, c_in,
     y_out, gf1_out, gp1_out, gf2_out, gp2_out,
-    wf1, wp1, wf2, wp2, xs, cs, ys, t1, s1, h1, c1,
+    wf1, wp1, wf2, wp2, xs, cs, ys,
     gf1, gp1, gf2, gp2, g32, gb, rb, lb, lr, ag,
     w_send, w_recv, w_own, x_send, x_recv, c_send, c_recv, y_send, y_recv, own,
     h_send, h_recv, l_send, l_recv, a_send, a_recv,
@@ -167,24 +167,45 @@
 
     rows = nhi * mc
 
-    def first_loop(k, carry):
+    def y_copy(j, k):
+        partner = flip(hi, j)
+        start = pl.multiple_of(hi * m + k * mc, mc)
+        part = pl.ds(pl.multiple_of(k * mc, mc), mc)
+        return remote(
+            ys.at[partner, part], y_out.at[pl.ds(start, mc)], y_send.at[j, k], y_recv.at[j, k],
+            "seqhi", partner,
+        )
+
+    def y_local(k):
+        start = pl.multiple_of(hi * m + k * mc, mc)
+        part = pl.ds(pl.multiple_of(k * mc, mc), mc)
+        return pltpu.make_async_copy(ys.at[hi, part], y_out.at[pl.ds(start, mc)], own.at[k])
+
+    def y_start(k):
+        for j in range(nhi - 1, 0, -1):
+            y_copy(j, k).start()
+        y_local(k).start()
+
+    def loop(k, carry):
         part = pl.ds(pl.multiple_of(k * mc, mc), mc)
         for j in range(1, nhi):
             x_copy(j, k).wait_recv()
         x = xs[:, part, :].reshape(rows, width)
         t, s = gates(mix(x, wf1, 1))
         hidden = (t * s).astype(BF16)
-        t1[k], s1[k], h1[k] = t, s, hidden
         x2 = (x.astype(F32) + dot(hidden, wp1[...])).astype(BF16)
-        t, s = gates(mix(x2, wf2, 2))
-        hidden = (t * s).astype(BF16)
+        t2, s2 = gates(mix(x2, wf2, 2))
+        hidden2 = (t2 * s2).astype(BF16)
         for j in range(1, nhi):
             c_copy(j, k).wait_recv()
+
         c = cs[:, part, :].reshape(rows, width)
-        c1[k] = back(x2, c, t, s, hidden, wf2, wp2, gf2, gp2, 2)
+        c = back(x2, c, t2, s2, hidden2, wf2, wp2, gf2, gp2, 2)
+        y = back(x, c, t, s, hidden, wf1, wp1, gf1, gp1, 1)
+        ys[:, part, :] = y.reshape(nhi, mc, width)
         return carry
 
-    lax.fori_loop(0, chunks, first_loop, 0)
+    lax.fori_loop(0, chunks, loop, 0)
 
     def pack(layer):
         gf, gp = (gf1, gp1) if layer == 0 else (gf2, gp2)
@@ -283,44 +304,16 @@
         steps.append(lambda: lo_finish(layer))
         return steps
 
-    def y_copy(j, k):
-        partner = flip(hi, j)
-        start = pl.multiple_of(hi * m + k * mc, mc)
-        part = pl.ds(pl.multiple_of(k * mc, mc), mc)
-        return remote(
-            ys.at[partner, part], y_out.at[pl.ds(start, mc)], y_send.at[j, k], y_recv.at[j, k],
-            "seqhi", partner,
-        )
-
-    def y_local(k):
-        start = pl.multiple_of(hi * m + k * mc, mc)
-        part = pl.ds(pl.multiple_of(k * mc, mc), mc)
-        return pltpu.make_async_copy(ys.at[hi, part], y_out.at[pl.ds(start, mc)], own.at[k])
-
-    pack(1)
-    hi_start(1, 0)
-    second = phases(1)
-
-    def second_loop(k, carry):
-        part = pl.ds(pl.multiple_of(k * mc, mc), mc)
-        x = xs[:, part, :].reshape(rows, width)
-        y = back(x, c1[k], t1[k], s1[k], h1[k], wf1, wp1, gf1, gp1, 1)
-        ys[:, part, :] = y.reshape(nhi, mc, width)
-        for j in range(nhi - 1, 0, -1):
-            y_copy(j, k).start()
-        y_local(k).start()
-        for i in range(min(len(second), chunks)):
-            pl.when(k == i)(second[i])
-        return carry
-
-    lax.fori_loop(0, chunks, second_loop, 0)
-
-    pack(0)
-    hi_start(0, 0)
-    for step in second[chunks:]:
-        step()
-    for step in phases(0):
-        step()
+    for layer in (1, 0):
+        pack(layer)
+        hi_start(layer, 0)
+    steps = [phases(1), phases(0)]
+    for at in range(stages + 1):
+        for side in steps:
+            side[at]()
+        if at == max(stages - 2, 0):
+            for late in range(chunks):
+                y_start(late)
     ag_finish(1)
     ag_finish(0)
 
@@ -353,7 +346,6 @@
     need = r * (h // 128) + rp * (width // 128)
     piece = -(-need // (16 * nlo)) * 16
     length = piece * nlo
-    rows = nhi * mc
     dma = pltpu.SemaphoreType.DMA
     any_spec = pl.BlockSpec(memory_space=pl.ANY)
     vmem = pl.BlockSpec(memory_space=pltpu.VMEM)
@@ -374,10 +366,6 @@
             pltpu.VMEM((nhi, m, width), BF16),
             pltpu.VMEM((nhi, m, width), BF16),
             pltpu.VMEM((nhi, m, width), BF16),
-            pltpu.VMEM((chunks, rows, h // 2), F32),
-            pltpu.VMEM((chunks, rows, h // 2), F32),
-            pltpu.VMEM((chunks, rows, h // 2), BF16),
-            pltpu.VMEM((chunks, rows, width), BF16),
             pltpu.VMEM((r * nhi, h), F32),
             pltpu.VMEM((rp * nhi, width), F32),
             pltpu.VMEM((r * nhi, h), F32),
@@ -397,7 +385,7 @@
             dma((2, nlo)), dma((2, nlo)),
         ],
         compiler_params=pltpu.CompilerParams(
-            collective_id=0, has_side_effects=True, vmem_limit_bytes=48 * 1024 * 1024
+            collective_id=0, has_side_effects=True, vmem_limit_bytes=62 * 1024 * 1024
         ),
         cost_estimate=pl.CostEstimate(
             flops=16 * samples * width * h * 2, bytes_accessed=8 * samples * width,

time: 84.3 us -> 70.7 us (0.84)
  Pallas kernels: 73.9 us -> 64.5 us
  local copies, waits for them, and re-layouts: 9.4 us -> 5.29 us
    pallas_call x1, Pallas kernels: 73.9 us -> 64.5 us  [local(): pl.pallas_call(functools.partial(kernel, nhi, nlo, chunks, scale), out_sh...]
    unnamed x17 -> x13, local copies, waits for them, and re-layouts: 9.4 us -> 5.29 us
where the time goes in v2:
time: 70.7 us; the launch traced here: 70.5 us
  Pallas kernels  64.5 us (91%)
  local copies, waits for them, and re-layouts  5.29 us (7%)
    pallas_call x1, Pallas kernels, local(): pl.pallas_call(functools.partial(kernel, nhi, nlo, chunks, scale), out_sh...  64.5 us
    unnamed x13, local copies, waits for them, and re-layouts  5.29 us

profile of v2, /device:TPU:0, one launch (start us, length us, event | category | flops | bytes accessed | tf_op | source)
XLA Modules:
  0.0 70.5 jit_solution(11394263480821369912)
XLA Ops:
  0.6 64.5 %shard_map.101 = (bf16[2048,256]{1,0:T(8,128)(2,1)}, f32[128,512]{1,0:T(8,128)}, f32[64,256]{1,0:T(8,128)}, f32[128,512]{1,0:T(8,128)}, f32[64,256]{1,0:T(8,128)}) custom-call(bf16[2048,256]{1,0:T(8,128)(2,1)} %x_in.1, bf16[128,512]{1,0:T(8,128)(2,1)} %f1_in.1, bf16[64,256]{1,0:T(8,128)(2,1)} %p1_in.1, bf16[128,512]{1,0:T(8,128)(2,1)} %f2_in.1, ...), custom_call_target="tpu_custom_call" | custom-call | flops 8589934592 | bytes 4194304 | tf_op jit(solution)/shard_map/pallas_call | solution.py:353
  65.2 0.0 copy-start.1
  65.2 2.3 %copy.16 = bf16[2048,256]{1,0:T(8,128)(2,1)} copy(bf16[2048,256]{1,0:T(8,128)(2,1)} %get-tuple-element.10) | data formatting | bytes 2097152
  67.5 0.0 copy-done.1
  67.5 0.0 copy-start.3
  67.5 0.0 copy-start
  67.5 0.7 copy.17
  68.2 0.2 copy-done.3
  68.3 0.6 copy.18
  69.0 0.0 copy-done
  69.0 0.0 copy-start.2
  69.0 0.7 copy.19
  69.7 0.2 copy-done.2
  69.8 0.6 copy.20
Async XLA Ops:
  65.2 2.3 %copy-start.1 = (f32[128,512]{1,0:T(8,128)S(1)}, f32[128,512]{1,0:T(8,128)}, u32[]{:S(2)}) copy-start(f32[128,512]{1,0:T(8,128)} %get-tuple-element.11) | copy-start | bytes 786436
  67.5 0.9 %copy-start.3 = (f32[64,256]{1,0:T(8,128)S(1)}, f32[64,256]{1,0:T(8,128)}, u32[]{:S(2)}) copy-start(f32[64,256]{1,0:T(8,128)} %get-tuple-element.12) | copy-start | bytes 196612
  67.5 1.5 %copy-start = (f32[128,512]{1,0:T(8,128)S(1)}, f32[128,512]{1,0:T(8,128)}, u32[]{:S(2)}) copy-start(f32[128,512]{1,0:T(8,128)} %get-tuple-element.13) | copy-start | bytes 786436
  69.0 0.9 %copy-start.2 = (f32[64,256]{1,0:T(8,128)S(1)}, f32[64,256]{1,0:T(8,128)}, u32[]{:S(2)}) copy-start(f32[64,256]{1,0:T(8,128)} %get-tuple-element.14) | copy-start | bytes 196612

commit v3 on v2

--- a/solution.py
+++ b/solution.py
@@ -42,7 +42,7 @@
     y_out, gf1_out, gp1_out, gf2_out, gp2_out,
     wf1, wp1, wf2, wp2, xs, cs, ys,
     gf1, gp1, gf2, gp2, g32, gb, rb, lb, lr, ag,
-    w_send, w_recv, w_own, x_send, x_recv, c_send, c_recv, y_send, y_recv, own,
+    w_send, w_recv, s_send, s_recv, w_own, x_send, x_recv, c_send, c_recv, y_send, y_recv, own,
     h_send, h_recv, l_send, l_recv, a_send, a_recv,
 ):
     hi, lo = lax.axis_index("seqhi"), lax.axis_index("seqlo")
@@ -93,11 +93,23 @@
             plan.append((h, b))
         held = held + [h ^ b for h in held]
 
+    part_rows = r // nlo
+    split = (0, 2) if nhi == 4 and r % (16 * nlo) == 0 else ()
+
+    def spread_copy(a, j):
+        start = pl.multiple_of(flip(hi, 2) * r + lo * part_rows, part_rows)
+        there = full[a].at[pl.ds(start, part_rows)]
+        return remote(there, there, s_send.at[a, j], s_recv.at[a, j], "seqlo", flip(lo, j))
+
     def weight_copy(a, at):
         h, b = plan[at]
         size = inputs[a].shape[0]
         there = pl.ds(pl.multiple_of(flip(hi, h) * size, size), size)
         src = inputs[a] if h == 0 else full[a].at[there]
+        if a in split and at == 0:
+            src = inputs[a].at[pl.ds(pl.multiple_of(lo * part_rows, part_rows), part_rows)]
+            start = pl.multiple_of(hi * size + lo * part_rows, part_rows)
+            there = pl.ds(start, part_rows)
         return remote(src, full[a].at[there], w_send.at[a, at], w_recv.at[a, at], "seqhi", flip(hi, b))
 
     def sample_copy(src, dst, send, recv, j, k):
@@ -112,15 +124,20 @@
     def c_copy(j, k):
         return sample_copy(c_in, cs, c_send, c_recv, j, k)
 
-    for a in range(4):
+    for a in (0, 2, 1, 3):
         for at in range(len(plan)):
             if plan[at][0] == 0:
                 weight_copy(a, at).start()
     for k in range(chunks):
-        for j in range(nhi - 1, 0, -1):
+        for j in (*range(2, nhi), 1):
             x_copy(j, k).start()
-        for j in range(nhi - 1, 0, -1):
+        for j in (*range(2, nhi), 1):
             c_copy(j, k).start()
+
+    for a in split:
+        weight_copy(a, 0).wait_recv()
+        for j in range(nlo - 1, 0, -1):
+            spread_copy(a, j).start()
 
     for ref in (gf1, gp1, gf2, gp2):
         ref[...] = jnp.zeros_like(ref)
@@ -130,9 +147,14 @@
 
     for copy in local_copies:
         copy.wait()
+    unread = []
     arrived = {h ^ b: at for at, (h, b) in enumerate(plan)}
     for a in range(4):
         waited = set()
+        if a in split:
+            waited.add(0)
+            for j in range(1, nlo):
+                spread_copy(a, j).wait_recv()
         for at, (h, b) in enumerate(plan):
             if h:
                 if arrived[h] not in waited:
@@ -141,7 +163,9 @@
                 weight_copy(a, at).start()
         for at in range(len(plan)):
             if at not in waited:
-                weight_copy(a, at).wait_recv()
+                unread.append((a, at))
+    for a, at in unread:
+        weight_copy(a, at).wait_recv()
 
     def gates(mixed):
         return jnp.tanh(mixed[:, :half]), sigmoid(mixed[:, half:])
@@ -320,6 +344,9 @@
     for a in range(4):
         for at in range(len(plan)):
             weight_copy(a, at).wait_send()
+    for a in split:
+        for j in range(1, nlo):
+            spread_copy(a, j).wait_send()
     for k in range(chunks):
         for j in range(1, nhi):
             x_copy(j, k).wait_send()
@@ -376,7 +403,7 @@
             pltpu.VMEM((2, length, 128), BF16),
             pltpu.VMEM((2, nlo, piece, 128), BF16),
             pltpu.VMEM((2, length, 128), BF16),
-            dma((4, nhi)), dma((4, nhi)), dma((6,)),
+            dma((4, nhi)), dma((4, nhi)), dma((4, nlo)), dma((4, nlo)), dma((6,)),
             dma((nhi, chunks)), dma((nhi, chunks)),
             dma((nhi, chunks)), dma((nhi, chunks)),
             dma((nhi, chunks)), dma((nhi, chunks)), dma((chunks,)),

time: 70.7 us -> 66.2 us (0.936)
  Pallas kernels: 64.5 us -> 60.1 us
    pallas_call x1, Pallas kernels: 64.5 us -> 60.1 us  [local(): pl.pallas_call(functools.partial(kernel, nhi, nlo, chunks, scale), out_sh...]
where the time goes in v3:
time: 66.2 us; the launch traced here: 66 us
  Pallas kernels  60.1 us (91%)
  local copies, waits for them, and re-layouts  5.29 us (8%)
    pallas_call x1, Pallas kernels, local(): pl.pallas_call(functools.partial(kernel, nhi, nlo, chunks, scale), out_sh...  60.1 us
    unnamed x13, local copies, waits for them, and re-layouts  5.29 us

profile of v3, /device:TPU:0, one launch (start us, length us, event | category | flops | bytes accessed | tf_op | source)
XLA Modules:
  0.0 66.0 jit_solution(3674746007788904548)
XLA Ops:
  0.6 60.1 %shard_map.101 = (bf16[2048,256]{1,0:T(8,128)(2,1)}, f32[128,512]{1,0:T(8,128)}, f32[64,256]{1,0:T(8,128)}, f32[128,512]{1,0:T(8,128)}, f32[64,256]{1,0:T(8,128)}) custom-call(bf16[2048,256]{1,0:T(8,128)(2,1)} %x_in.1, bf16[128,512]{1,0:T(8,128)(2,1)} %f1_in.1, bf16[64,256]{1,0:T(8,128)(2,1)} %p1_in.1, bf16[128,512]{1,0:T(8,128)(2,1)} %f2_in.1, ...), custom_call_target="tpu_custom_call" | custom-call | flops 8589934592 | bytes 4194304 | tf_op jit(solution)/shard_map/pallas_call | solution.py:380
  60.7 0.0 copy-start.1
  60.7 2.3 %copy.16 = bf16[2048,256]{1,0:T(8,128)(2,1)} copy(bf16[2048,256]{1,0:T(8,128)(2,1)} %get-tuple-element.10) | data formatting | bytes 2097152
  63.0 0.0 copy-done.1
  63.0 0.0 copy-start.3
  63.0 0.0 copy-start
  63.0 0.7 %copy.17 = f32[128,512]{1,0:T(8,128)} copy(f32[128,512]{1,0:T(8,128)S(1)} %copy-done.1) | data formatting | bytes 524288
  63.7 0.2 copy-done.3
  63.9 0.6 copy.18
  64.5 0.0 copy-done
  64.5 0.0 copy-start.2
  64.5 0.7 %copy.19 = f32[128,512]{1,0:T(8,128)} copy(f32[128,512]{1,0:T(8,128)S(1)} %copy-done) | data formatting | bytes 524288
  65.2 0.2 copy-done.2
  65.4 0.6 copy.20
Async XLA Ops:
  60.7 2.3 %copy-start.1 = (f32[128,512]{1,0:T(8,128)S(1)}, f32[128,512]{1,0:T(8,128)}, u32[]{:S(2)}) copy-start(f32[128,512]{1,0:T(8,128)} %get-tuple-element.11) | copy-start | bytes 786436
  63.0 0.9 %copy-start.3 = (f32[64,256]{1,0:T(8,128)S(1)}, f32[64,256]{1,0:T(8,128)}, u32[]{:S(2)}) copy-start(f32[64,256]{1,0:T(8,128)} %get-tuple-element.12) | copy-start | bytes 196612
  63.0 1.5 %copy-start = (f32[128,512]{1,0:T(8,128)S(1)}, f32[128,512]{1,0:T(8,128)}, u32[]{:S(2)}) copy-start(f32[128,512]{1,0:T(8,128)} %get-tuple-element.13) | copy-start | bytes 786436
  64.5 0.9 %copy-start.2 = (f32[64,256]{1,0:T(8,128)S(1)}, f32[64,256]{1,0:T(8,128)}, u32[]{:S(2)}) copy-start(f32[64,256]{1,0:T(8,128)} %get-tuple-element.14) | copy-start | bytes 196612
